TPU v7x, 32 devices: a whole 2x2x4 slice. The times are simulated.
32 devices in a mesh: rep: 2 (over y), srv: 2 (over x), tp: 8 (over z, core).
Axes of the slice: x: 2, y: 2, z: 4, core: 2. Of those that a mesh axis runs over, the one named last changes fastest.
Arguments:
- tokens: bfloat16 [2, 160, 8192], P(None, ('rep', 'srv'), 'tp'), parts along dimension 1, may hold values from -6 to 6
- input_norm_gain: bfloat16 [8192], P('tp'), may hold values from 0.25 to 1.75
- query_weight: bfloat16 [8192, 8192], P(None, 'tp'), may hold values from -0.0625 to 0.0625
- key_weight: bfloat16 [8192, 1024], P(None, 'tp'), may hold values from -0.0625 to 0.0625
- value_weight: bfloat16 [8192, 1024], P(None, 'tp'), may hold values from -0.0625 to 0.0625
- output_weight: bfloat16 [8192, 8192], P('tp'), may hold values from -0.0625 to 0.0625
- adapter_down_maps: bfloat16 [8, 8192, 128], P('srv', 'tp'), may hold values from -0.0625 to 0.0625
- adapter_query_up: bfloat16 [8, 64, 8192], P('srv', None, 'tp'), may hold values from -0.75 to 0.75
- adapter_value_up: bfloat16 [8, 64, 1024], P('srv', None, 'tp'), may hold values from -0.75 to 0.75
- key_value_cache: bfloat16 [160, 128, 2, 1024], P(('rep', 'srv', 'tp')), parts along dimension 0, may hold values from -480 to 480, as said below
- cached_length: int32 [160], P(('rep', 'srv', 'tp')), parts along dimension 0, may hold values from 1 to 128, as said below
- request_adapter_entry: int32 [160], P(('rep', 'srv')), parts along dimension 0, may hold values from 0 to 2
- group_adapter_ids: int32 [2, 3], replicated, may hold values from 0 to 7, as said below
- adapter_slot_table: int32 [8], replicated, may hold values from 0 to 7, as said below
Outputs:
- mixed: bfloat16 [2, 160, 8192], P(None, ('rep', 'srv'), 'tp'), parts along dimension 1
There are 2 independent parts, one for each index of `rep`. A program takes and returns all parts, laid end to end along the dimension named above; an argument that names none is the same for every part. Nothing has to cross between parts.
Inputs may be any that keep to these rules, and one draw needn't show every extreme that they name: `request_adapter_entry`: index into the request's group's row of group_adapter_ids. `group_adapter_ids`: each row lists 3 different adapter ids. Adapter a is stored at slot adapter_slot_table[a] of adapter_down_maps, adapter_query_up and adapter_value_up; every slot once. The new tokens of a request sit at positions cached_length and cached_length + 1. `key_value_cache`: keys are stored with the rotary embedding already applied.
All inputs are finite; a program needn't handle non-finite values.
Results may differ from a plain program's by a relative error of at most 0.011.
Values may be sent and summed in bfloat16 or wider, within the bound.
A program may use at most 128 MiB of HBM per device.

v0:
```python
import math

import jax
import jax.numpy as jnp
from jax import lax
from jax.sharding import PartitionSpec as P

KV_HEADS = 8
HEAD = 128
STEPS = 2


def normalize(values, gain):
    wide = values.astype(jnp.float32)
    scale = lax.rsqrt(jnp.mean(wide * wide, axis=-1, keepdims=True) + 1e-05)
    return (wide * scale * gain.astype(jnp.float32)).astype(jnp.bfloat16)


def rotate(block, position):
    half = block.shape[-1] // 2
    freq = jnp.exp(
        -(jnp.arange(half).astype(jnp.float32) * 2.0 / block.shape[-1]) * math.log(500000.0)
    )
    angle = position.astype(jnp.float32)[:, None, None] * freq
    cosine = jnp.cos(angle)
    sine = jnp.sin(angle)
    first = block[..., :half]
    second = block[..., half:]
    return jnp.concatenate(
        [first * cosine - second * sine, second * cosine + first * sine], axis=-1
    )


def attend(query, cache, length, new_keys, new_values):
    rows = query.shape[0]
    span = cache.shape[1]
    fresh = new_keys.shape[1]
    group = query.shape[1] // (KV_HEADS * HEAD)
    grouped = query.reshape(rows, KV_HEADS, group, HEAD)
    old_keys = cache[:, :, 0].reshape(rows, span, KV_HEADS, HEAD)
    old_values = cache[:, :, 1].reshape(rows, span, KV_HEADS, HEAD)
    keys_new = new_keys.reshape(rows, fresh, KV_HEADS, HEAD)
    values_new = new_values.reshape(rows, fresh, KV_HEADS, HEAD)
    factor = HEAD ** (-0.5)
    old_scores = (
        jnp.einsum("rkgd,rpkd->rkgp", grouped, old_keys, preferred_element_type=jnp.float32)
        * factor
    )
    valid = jnp.arange(span)[None, :] < length[:, None]
    old_scores = jnp.where(valid[:, None, None, :], old_scores, -jnp.inf)
    new_scores = (
        jnp.einsum("rkgd,rskd->rkgs", grouped, keys_new, preferred_element_type=jnp.float32)
        * factor
    )
    top = jnp.maximum(
        jnp.max(old_scores, axis=-1, keepdims=True), jnp.max(new_scores, axis=-1, keepdims=True)
    )
    old_exp = jnp.exp(old_scores - top)
    new_exp = jnp.exp(new_scores - top)
    total = jnp.sum(old_exp, axis=-1, keepdims=True) + jnp.sum(new_exp, axis=-1, keepdims=True)
    old_weight = (old_exp / total).astype(jnp.bfloat16)
    new_weight = (new_exp / total).astype(jnp.bfloat16)
    result = jnp.einsum(
        "rkgp,rpkd->rkgd", old_weight, old_values, preferred_element_type=jnp.float32
    )
    result = result + jnp.einsum(
        "rkgs,rskd->rkgd", new_weight, values_new, preferred_element_type=jnp.float32
    )
    return result.reshape(rows, KV_HEADS * group * HEAD).astype(jnp.bfloat16)


def on_device(
    tokens,
    input_norm_gain,
    query_weight,
    key_weight,
    value_weight,
    output_weight,
    adapter_down_maps,
    adapter_query_up,
    adapter_value_up,
    key_value_cache,
    cached_length,
    request_adapter_entry,
    group_adapter_ids,
    adapter_slot_table,
):
    group_index = lax.axis_index("srv")
    need = group_adapter_ids.shape[1]
    every = (
        lax.all_gather(adapter_down_maps, "srv", axis=0, tiled=True),
        lax.all_gather(adapter_query_up, "srv", axis=0, tiled=True),
        lax.all_gather(adapter_value_up, "srv", axis=0, tiled=True),
    )
    wanted = adapter_slot_table[group_adapter_ids[group_index]]
    down_need = jnp.take(every[0], wanted, axis=0)
    up_query_need = jnp.take(every[1], wanted, axis=0)
    up_value_need = jnp.take(every[2], wanted, axis=0)
    picks = (request_adapter_entry[:, None] == jnp.arange(need)[None, :]).astype(jnp.float32)
    rank = up_query_need.shape[1]

    def attend_step(step, query_rows, key_steps, value_steps):
        rows = query_rows.shape[0]
        turned = (
            rotate(query_rows.astype(jnp.float32).reshape(rows, -1, HEAD), cached_length + step)
            .astype(jnp.bfloat16)
            .reshape(rows, -1)
        )
        fresh_keys = jnp.stack(
            [
                rotate(key_steps[s].astype(jnp.float32).reshape(rows, -1, HEAD), cached_length + s)
                .astype(jnp.bfloat16)
                .reshape(rows, -1)
                for s in range(step + 1)
            ],
            axis=1,
        )
        fresh_values = jnp.stack([value_steps[s] for s in range(step + 1)], axis=1)
        return attend(turned, key_value_cache, cached_length, fresh_keys, fresh_values)

    steps_here = tokens.shape[0]
    width = tokens.shape[2]
    flat = tokens.reshape(-1, width)
    whole = lax.all_gather(flat, "tp", axis=1, tiled=True)
    gain = lax.all_gather(input_norm_gain, "tp", axis=0, tiled=True)
    normed_input = normalize(whole, gain)
    mine = lax.dynamic_slice_in_dim(normed_input, lax.axis_index("tp") * width, width, 1)
    row_picks = jnp.tile(picks, (steps_here, 1))[:, :, None]
    partial_value = jnp.einsum("md,ndk->mnk", mine, down_need, preferred_element_type=jnp.float32)
    shrunk = jnp.sum(partial_value * row_picks, axis=1)
    rank_row_values = lax.psum(shrunk, "tp").astype(jnp.bfloat16)
    query_lift = jnp.einsum(
        "mk,nkc->mnc", rank_row_values[:, :rank], up_query_need, preferred_element_type=jnp.float32
    )
    value_lift = jnp.einsum(
        "mk,nkc->mnc", rank_row_values[:, rank:], up_value_need, preferred_element_type=jnp.float32
    )
    query = (
        jnp.dot(normed_input, query_weight, preferred_element_type=jnp.float32)
        + jnp.sum(query_lift * row_picks, axis=1)
    ).astype(jnp.bfloat16)
    keys = jnp.dot(normed_input, key_weight, preferred_element_type=jnp.float32).astype(
        jnp.bfloat16
    )
    values = (
        jnp.dot(normed_input, value_weight, preferred_element_type=jnp.float32)
        + jnp.sum(value_lift * row_picks, axis=1)
    ).astype(jnp.bfloat16)

    def by_step(array):
        return array.reshape(steps_here, -1, array.shape[1])

    query, keys, values = (
        lax.all_to_all(by_step(query), "tp", split_axis=1, concat_axis=2, tiled=True),
        lax.all_to_all(by_step(keys), "tp", split_axis=1, concat_axis=2, tiled=True),
        lax.all_to_all(by_step(values), "tp", split_axis=1, concat_axis=2, tiled=True),
    )
    attended = [attend_step(step, query[step], keys, values) for step in range(STEPS)]
    finish_attended = jnp.stack(attended)
    heads = lax.all_to_all(finish_attended, "tp", split_axis=2, concat_axis=1, tiled=True)
    flat_heads = heads.reshape(-1, heads.shape[2])
    summed = lax.psum_scatter(
        lax.dot_general(
            output_weight, flat_heads, (((0,), (1,)), ((), ())), preferred_element_type=jnp.float32
        ),
        "tp",
        scatter_dimension=0,
        tiled=True,
    )
    return (tokens.astype(jnp.float32) + summed.T.reshape(tokens.shape)).astype(jnp.bfloat16)


def solution(mesh):
    placed = (
        P(None, ("rep", "srv"), "tp"),
        P("tp"),
        P(None, "tp"),
        P(None, "tp"),
        P(None, "tp"),
        P("tp", None),
        P("srv", "tp", None),
        P("srv", None, "tp"),
        P("srv", None, "tp"),
        P(("rep", "srv", "tp"), None, None, None),
        P(("rep", "srv", "tp")),
        P(("rep", "srv")),
        P(),
        P(),
    )
    return jax.shard_map(
        on_device,
        mesh=mesh,
        in_specs=placed,
        out_specs=P(None, ("rep", "srv"), "tp"),
        check_vma=False,
    )
```

profile of v0, /device:TPU:0, one launch (start us, length us, event | category | flops | bytes accessed | tf_op | source)
XLA Modules:
  0.0 288.3 jit_solution(3091007098450566572)
XLA Ops:
  6.5 0.7 all-gather.8.cloned.1.call-update
  7.3 0.7 all-gather.6.cloned.1.call-update
  8.1 0.7 all-gather.4.cloned.1.call-update
  8.7 0.7 fusion.55
  9.5 14.5 %all_gather.16 = bf16[8192]{0:T(1024)(128)(2,1)S(1)} all-gather(bf16[1024]{0:T(1024)(128)(2,1)} %param.15), channel_id=1, replica_groups=mesh['rep'=2,'srv'=2,'tp'=8] {'tp'}, dimensions={0}, use_global_device_ids=true | all-gather | bytes 18432 | tf_op jit(solution)/shard_map/all_gather | solution.py:125
  24.0 8.4 %fusion.67 = (bf16[5,128,1,1024]{3,2,1,0:T(2,128)(2,1)}, bf16[5,128,1,1024]{3,2,1,0:T(2,128)(2,1)}) fusion(bf16[5,128,2,1024]{3,2,1,0:T(2,128)(2,1)} %param.23), kind=kLoop, calls=%fused_computation.134 | loop fusion | bytes 5242880 | tf_op jit(solution)/shard_map/slice | solution.py:41
  32.4 6.1 %copy.249 = bf16[5,128,1,1024]{1,3,0,2:T(8,128)(2,1)} copy(bf16[5,128,1,1024]{3,2,1,0:T(2,128)(2,1)} %get-tuple-element.5) | data formatting | bytes 2621440
  38.5 6.3 %copy.248 = bf16[5,128,1,1024]{1,3,0,2:T(8,128)(2,1)} copy(bf16[5,128,1,1024]{3,2,1,0:T(2,128)(2,1)} %get-tuple-element.6) | data formatting | bytes 2621440
  44.8 0.6 gather_fusion
  45.5 6.8 %all_gather.19 = bf16[8,64,128]{2,1,0:T(8,128)(2,1)S(1)} all-gather(bf16[4,64,128]{2,1,0:T(8,128)(2,1)S(1)} %copy-done.8), channel_id=1, replica_groups=mesh['rep'=2,'srv'=2,'tp'=8] {'srv'}, dimensions={0}, use_global_device_ids=true | all-gather | bytes 196608 | tf_op jit(solution)/shard_map/all_gather | solution.py:93
  52.3 0.6 gather_fusion.3
  53.1 2.6 gather_fusion.2
  55.7 13.4 %all-gather.6.cloned.1.call-done = bf16[8,1024,128]{2,1,0:T(8,128)(2,1)} async-done(((bf16[4,1024,128]{2,1,0:T(8,128)(2,1)}), bf16[8,1024,128]{2,1,0:T(8,128)(2,1)}) %all-gather.6.cloned.1.call-update) | async-done | bytes 2097168 | tf_op jit(solution)/shard_map/all_gather | solution.py:91
  69.0 3.2 %gather_fusion.1 = bf16[3,1024,128]{2,1,0:T(8,128)(2,1)} fusion(bf16[8,1024,128]{2,1,0:T(8,128)(2,1)} %all-gather.6.cloned.1.call-done, s32[1024]{0:T(1024)S(1)} %pad_clamp_fusion), kind=kCustom, calls=%fused_computation.1 | custom fusion | bytes 1572876 | tf_op jit(solution)/shard_map/jit(_take)/gather | solution.py:96
  72.2 21.9 %all-gather.4.cloned.1.call-done = bf16[80,8192]{1,0:T(8,128)(2,1)} async-done(((bf16[80,1024]{1,0:T(8,128)(2,1)}), bf16[80,8192]{1,0:T(8,128)(2,1)}) %all-gather.4.cloned.1.call-update) | async-done | bytes 1310736 | tf_op jit(solution)/shard_map/all_gather | solution.py:124
  94.1 1.8 fusion
  95.9 0.4 fusion.2
  96.3 0.5 convolution_convert_fusion
  96.9 0.6 copy.222
  97.5 3.3 %all-to-all-start.1 = ((bf16[2,40,128]{2,0,1:T(2,128)(2,1)}), bf16[2,40,128]{2,0,1:T(2,128)(2,1)S(1)}, u32[]{:S(2)}, u32[]{:S(2)}) async-start(bf16[2,40,128]{2,0,1:T(2,128)(2,1)} %copy.222), calls=%async_computation.1 | async-start | bytes 40960 | tf_op jit(solution)/shard_map/all_to_all | solution.py:155
  100.8 1.5 fusion.9
  102.4 29.7 %psum.7 = bf16[80,128]{0,1:T(8,128)(2,1)S(1)} all-reduce(f32[80,128]{0,1:T(8,128)S(1)} %copy.217), channel_id=1, replica_groups=mesh['rep'=2,'srv'=2,'tp'=8] {'tp'}, use_global_device_ids=true, to_apply=%region_2.3 | all-reduce | flops 10240 | bytes 61440 | tf_op jit(solution)/shard_map/psum | solution.py:131
  132.1 1.4 fusion.3
  133.7 8.9 %fusion.4 = bf16[80,1024]{1,0:T(8,128)(2,1)S(1)} fusion(f32[80,1024]{1,0:T(8,128)S(1)} %fusion.3, bf16[80,8192]{1,0:T(8,128)(2,1)S(1)} %fusion.2, bf16[8192,1024]{1,0:T(8,128)(2,1)} %param.16), kind=kOutput, calls=%fused_computation.14 | convolution fusion | flops 1342341120 | bytes 18579456 | tf_op jit(solution)/shard_map/dot_general | solution.py:139
  142.7 0.5 fusion.11
  143.2 0.8 copy.218
  144.0 0.6 copy.226
  144.7 3.3 %all-to-all-start.2 = ((bf16[2,40,128]{2,0,1:T(2,128)(2,1)}), bf16[2,40,128]{2,0,1:T(2,128)(2,1)S(1)}, u32[]{:S(2)}, u32[]{:S(2)}) async-start(bf16[2,40,128]{2,0,1:T(2,128)(2,1)} %copy.226), calls=%async_computation.2 | async-start | bytes 40960 | tf_op jit(solution)/shard_map/all_to_all | solution.py:156
  148.3 5.3 %all-to-all-done.2 = bf16[2,40,128]{2,0,1:T(2,128)(2,1)S(1)} async-done(((bf16[2,40,128]{2,0,1:T(2,128)(2,1)}), bf16[2,40,128]{2,0,1:T(2,128)(2,1)S(1)}, u32[]{:S(2)}, u32[]{:S(2)}) %all-to-all-start.2) | async-done | bytes 20512 | tf_op jit(solution)/shard_map/all_to_all | solution.py:156
  153.6 3.4 %all-to-all-start = ((bf16[2,40,1024]{2,0,1:T(2,128)(2,1)}), bf16[2,40,1024]{2,0,1:T(2,128)(2,1)S(1)}, u32[]{:S(2)}, u32[]{:S(2)}) async-start(bf16[2,40,1024]{2,0,1:T(2,128)(2,1)} %copy.218), calls=%async_computation | async-start | bytes 327680 | tf_op jit(solution)/shard_map/all_to_all | solution.py:154
  157.2 0.6 bitcast_convert_fusion
  158.0 6.2 %all-to-all-done = bf16[2,40,1024]{2,0,1:T(2,128)(2,1)S(1)} async-done(((bf16[2,40,1024]{2,0,1:T(2,128)(2,1)}), bf16[2,40,1024]{2,0,1:T(2,128)(2,1)S(1)}, u32[]{:S(2)}, u32[]{:S(2)}) %all-to-all-start) | async-done | bytes 163872 | tf_op jit(solution)/shard_map/all_to_all | solution.py:154
  164.7 0.6 fusion.71
  165.6 0.6 fusion.69
  166.2 0.3 fusion.70
  166.8 0.8 fusion.7
  167.8 0.2 fusion.34
  168.0 0.8 fusion.8
  169.0 6.9 %copy.237 = bf16[1,5,8192]{1,0,2:T(2,128)(2,1)} copy(bf16[1,5,8192]{2,1,0:T(8,128)(2,1)S(1)} %convert_element_type.176) | data formatting | bytes 163840 | tf_op jit(solution)/shard_map/convert_element_type | solution.py:69
  175.8 6.8 %copy.236 = bf16[1,5,8192]{1,0,2:T(2,128)(2,1)} copy(bf16[1,5,8192]{2,1,0:T(8,128)(2,1)S(1)} %convert_element_type.167) | data formatting | bytes 163840 | tf_op jit(solution)/shard_map/convert_element_type | solution.py:69
  182.7 13.3 %fusion.72 = bf16[8192,2,5]{2,1,0:T(2,128)(2,1)} fusion(bf16[1,5,8192]{1,0,2:T(2,128)(2,1)} %copy.237, bf16[1,5,8192]{1,0,2:T(2,128)(2,1)} %copy.236), kind=kLoop, calls=%fused_computation.139 | loop fusion | flops 327680 | bytes 327680
  196.0 6.9 %reshape.447 = bf16[8,2,5120]{2,1,0:T(2,128)(2,1)S(1)} reshape(bf16[8192,2,5]{2,1,0:T(2,128)(2,1)} %fusion.72) | data formatting | bytes 327680
  202.9 9.9 %all_to_all.60 = bf16[8,2,5120]{2,1,0:T(2,128)(2,1)S(1)} all-to-all(bf16[8,2,5120]{2,1,0:T(2,128)(2,1)S(1)} %reshape.447), channel_id=1, replica_groups=mesh['rep'=2,'srv'=2,'tp'=8] {'tp'}, dimensions={0} | all-to-all | bytes 327680 | tf_op jit(solution)/shard_map/all_to_all | solution.py:160
  212.8 10.1 %reshape.448 = bf16[8192,2,5]{2,1,0:T(2,128)(2,1)} reshape(bf16[8,2,5120]{2,1,0:T(2,128)(2,1)S(1)} %all_to_all.60) | data formatting | bytes 327680
  222.9 9.7 %copy.247 = bf16[2,5,8,1024]{3,1,2,0:T(8,128)(2,1)S(1)} copy(bf16[2,5,8,1024]{1,0,3,2:T(2,128)(2,1)} %bitcast.103) | data formatting | bytes 327680 | tf_op jit(solution)/shard_map/all_to_all | solution.py:160
  232.7 10.4 %convolution_bitcast_fusion = f32[8192,80]{0,1:T(8,128)} fusion(bf16[80,1024]{1,0:T(8,128)(2,1)S(1)} %reshape.403, bf16[1024,8192]{1,0:T(8,128)(2,1)} %param.19), kind=kOutput, calls=%fused_computation.4 | convolution fusion | flops 1342177280 | bytes 19562496 | tf_op jit(solution)/shard_map/dot_general | solution.py:163
  243.1 36.9 %reduce-scatter.2.cloned.1.call-done = f32[1024,80]{0,1:T(8,128)} async-done(((f32[8192,80]{0,1:T(8,128)}), f32[1024,80]{0,1:T(8,128)}) %reduce-scatter.2.cloned.1.call-update) | async-done | bytes 327696 | tf_op jit(solution)/shard_map/reduce_scatter | solution.py:162
  280.1 1.7 add_convert_fusion
  (74 shorter events, 2.8 us)
Async XLA Ops:
  6.5 89.8 %copy-start = (bf16[8192,128]{1,0:T(8,128)(2,1)S(1)}, bf16[8192,128]{1,0:T(8,128)(2,1)}, u32[]{:S(2)}) copy-start(bf16[8192,128]{1,0:T(8,128)(2,1)} %param.17) | copy-start | bytes 6291460
  6.5 46.5 %all-gather.8.cloned.1.call-start = ((), (), s32[]{:S(2)}) async-start(), calls=%async_computation.7 | async-start | bytes 1572864 | tf_op jit(solution)/shard_map/all_gather | solution.py:92
  7.3 61.8 %all-gather.6.cloned.1.call-start = ((), (), s32[]{:S(2)}) async-start(), calls=%async_computation.6 | async-start | bytes 3145728 | tf_op jit(solution)/shard_map/all_gather | solution.py:91
  8.0 86.1 %all-gather.4.cloned.1.call-start = ((), (), s32[]{:S(2)}) async-start(), calls=%async_computation.5 | async-start | bytes 1474560 | tf_op jit(solution)/shard_map/all_gather | solution.py:124
  38.5 6.3 %copy-start.10 = (s32[2,3]{1,0:T(2,128)S(1)}, s32[2,3]{1,0:T(2,128)}, u32[]{:S(2)}) copy-start(s32[2,3]{1,0:T(2,128)} %param.26) | copy-start | bytes 76
  38.5 6.3 %copy-start.2 = (s32[8]{0:T(128)S(1)}, s32[8]{0:T(128)}, u32[]{:S(2)}) copy-start(s32[8]{0:T(128)} %param.27) | copy-start | bytes 100
  38.5 6.9 %copy-start.8 = (bf16[4,64,128]{2,1,0:T(8,128)(2,1)S(1)}, bf16[4,64,128]{2,1,0:T(8,128)(2,1)}, u32[]{:S(2)}) copy-start(bf16[4,64,128]{2,1,0:T(8,128)(2,1)} %param.22) | copy-start | bytes 196612
  38.5 14.3 %copy-start.11 = (s32[5]{0:T(128)S(1)}, s32[5]{0:T(128)}, u32[]{:S(2)}) copy-start(s32[5]{0:T(128)} %param.24) | copy-start | bytes 64
  94.1 1.8 copy-start.4
  97.5 47.2 %all-to-all-start.1 = ((bf16[2,40,128]{2,0,1:T(2,128)(2,1)}), bf16[2,40,128]{2,0,1:T(2,128)(2,1)S(1)}, u32[]{:S(2)}, u32[]{:S(2)}) async-start(bf16[2,40,128]{2,0,1:T(2,128)(2,1)} %copy.222), calls=%async_computation.1 | async-start | bytes 40960 | tf_op jit(solution)/shard_map/all_to_all | solution.py:155
  133.7 8.9 %copy-start.6 = (bf16[8192,128]{1,0:T(8,128)(2,1)S(1)}, bf16[8192,128]{1,0:T(8,128)(2,1)}, u32[]{:S(2)}) copy-start(bf16[8192,128]{1,0:T(8,128)(2,1)} %param.18) | copy-start | bytes 6291460
  143.2 21.5 %copy-start.3 = (bf16[5,128,1,1024]{1,3,0,2:T(8,128)(2,1)S(1)}, bf16[5,128,1,1024]{1,3,0,2:T(8,128)(2,1)}, u32[]{:S(2)}) copy-start(bf16[5,128,1,1024]{1,3,0,2:T(8,128)(2,1)} %copy.248) | copy-start | bytes 3932164
  144.7 8.9 %all-to-all-start.2 = ((bf16[2,40,128]{2,0,1:T(2,128)(2,1)}), bf16[2,40,128]{2,0,1:T(2,128)(2,1)S(1)}, u32[]{:S(2)}, u32[]{:S(2)}) async-start(bf16[2,40,128]{2,0,1:T(2,128)(2,1)} %copy.226), calls=%async_computation.2 | async-start | bytes 40960 | tf_op jit(solution)/shard_map/all_to_all | solution.py:156
  153.6 10.5 %all-to-all-start = ((bf16[2,40,1024]{2,0,1:T(2,128)(2,1)}), bf16[2,40,1024]{2,0,1:T(2,128)(2,1)S(1)}, u32[]{:S(2)}, u32[]{:S(2)}) async-start(bf16[2,40,1024]{2,0,1:T(2,128)(2,1)} %copy.218), calls=%async_computation | async-start | bytes 327680 | tf_op jit(solution)/shard_map/all_to_all | solution.py:154
  157.0 123.1 %reduce-scatter.2.cloned.1.call-start = ((), (), s32[]{:S(2)}) async-start(), calls=%async_computation.8 | async-start | bytes 2949120 | tf_op jit(solution)/shard_map/reduce_scatter | solution.py:162
  164.7 2.1 copy-start.5
  164.7 2.1 copy-start.9
  232.6 49.1 %copy-start.1 = (bf16[8192,128]{1,0:T(8,128)(2,1)S(1)}, bf16[8192,128]{1,0:T(8,128)(2,1)}, u32[]{:S(2)}) copy-start(bf16[8192,128]{1,0:T(8,128)(2,1)} %param.17) | copy-start | bytes 6291460
  243.1 37.0 %copy-start.7 = (bf16[2,40,1024]{2,1,0:T(8,128)(2,1)S(1)}, bf16[2,40,1024]{2,1,0:T(8,128)(2,1)}, u32[]{:S(2)}) copy-start(bf16[2,40,1024]{2,1,0:T(8,128)(2,1)} %param.14) | copy-start | bytes 491524
Sparse Core Ops, SparseCore 0:
  8.9 23.9 all-gather.7
  34.5 34.5 all-gather.5
  70.6 23.4 all-gather.3
  243.3 36.7 reduce-scatter.1
where the time goes:
time: 290 us; the launch traced here: 288 us
  waiting for transfers between devices  85.9 us (30%)
  local copies, waits for them, and re-layouts  70.8 us (24%)
  blocking collectives  60.9 us (21%)
  matrix products  27.1 us (9%)
  other arithmetic  19.7 us (7%)
  between operations  13.6 us (5%)
  starting transfers between devices  10.3 us (4%)
    reduce_scatter x1, waiting for transfers between devices, on_device(): lax.psum_scatter(lax.dot_general(output_weight, flat_heads, (((0,), (1,))...  36.9 us
    psum x1, blocking collectives, on_device(): rank_row_values = lax.psum(shrunk, 'tp').astype(jnp.bfloat16)  29.7 us
    unnamed x28, local copies, waits for them, and re-layouts  29.4 us
    all_gather x1, waiting for transfers between devices, on_device(): whole = lax.all_gather(flat, 'tp', axis=1, tiled=True)  21.9 us
    all_gather x1, blocking collectives, on_device(): gain = lax.all_gather(input_norm_gain, 'tp', axis=0, tiled=True)  14.5 us
    convert_element_type x4, local copies, waits for them, and re-layouts, attend(): return result.reshape(rows, KV_HEADS * group * HEAD).astype(jnp.bfloat16)  13.9 us
    all_gather x1, waiting for transfers between devices, on_device(): lax.all_gather(adapter_down_maps, 'srv', axis=0, tiled=True)  13.4 us
    unnamed x1, other arithmetic  13.3 us
  transfers between devices with their start and end apart: 7, of which 5 were waited for; matrix products, arithmetic and copies ran while one was open for 15% of the time, Pallas kernels for 0%

commit v1 on v0

--- a/solution.py
+++ b/solution.py
@@ -1,13 +1,20 @@
+import functools
 import math
 
 import jax
 import jax.numpy as jnp
 from jax import lax
+from jax.experimental import pallas as pl
+from jax.experimental.pallas import tpu as pltpu
 from jax.sharding import PartitionSpec as P
 
 KV_HEADS = 8
 HEAD = 128
 STEPS = 2
+CORES = 2
+MESH = pl.DeviceIdType.MESH
+F32 = jnp.float32
+BF16 = jnp.bfloat16
 
 
 def normalize(values, gain):
@@ -170,6 +177,660 @@
     return (tokens.astype(jnp.float32) + summed.T.reshape(tokens.shape)).astype(jnp.bfloat16)
 
 
+def remote(src, dst, send, recv, device):
+    return pltpu.make_async_remote_copy(
+        src_ref=src,
+        dst_ref=dst,
+        send_sem=send,
+        recv_sem=recv,
+        device_id=device,
+        device_id_type=MESH,
+    )
+
+
+def iota(shape, axis):
+    return lax.broadcasted_iota(jnp.int32, shape, axis)
+
+
+def dot(left, right):
+    return jnp.dot(left, right, preferred_element_type=F32)
+
+
+def block_kernel(
+    sizes,
+    tokens_ref,
+    gain_ref,
+    entry_ref,
+    ids_ref,
+    table_ref,
+    length_ref,
+    query_w,
+    key_w,
+    value_w,
+    out_w,
+    down_hbm,
+    up_query_hbm,
+    up_value_hbm,
+    cache_hbm,
+    out_ref,
+    weight,
+    wide_out,
+    down,
+    up,
+    cache,
+    pairs,
+    gathered,
+    xs,
+    masks,
+    squares,
+    acc,
+    half_send,
+    half_recv,
+    chip_sum,
+    ranks,
+    lift_own,
+    lift_send,
+    lift_recv,
+    heads_send,
+    heads_recv,
+    turned,
+    results,
+    back_send,
+    back_recv,
+    own_part,
+    sib_send,
+    sib_recv,
+    sum_send,
+    sum_recv,
+    weight_sem,
+    wide_sem,
+    small_sem,
+    cache_sem,
+    x_send,
+    x_recv,
+    forward_send,
+    peer_send,
+    peer_recv,
+    square_send,
+    square_recv,
+    half_sem,
+    chip_send,
+    chip_recv,
+    rank_sem,
+    lift_sem,
+    heads_ssem,
+    heads_rsem,
+    back_ssem,
+    back_rsem,
+    sib_ssem,
+    sib_rsem,
+    sum_ssem,
+    sum_rsem,
+):
+    T, requests, here, owned, need = sizes
+    chips = T // CORES
+    rows = STEPS * requests
+    width = tokens_ref.shape[2]
+    columns = query_w.shape[1]
+    group = columns // HEAD
+    pad = 16
+    me = lax.axis_index("tp")
+    side = lax.axis_index("srv")
+    z = me // CORES
+    core = lax.rem(me, CORES)
+    sibling = z * CORES + (1 - core)
+    other = 1 - side
+
+    def tp(index):
+        return {"tp": index}
+
+    def at_chip(k):
+        return lax.rem(z + k, chips)
+
+    peer = {"srv": other}
+
+    def weight_copies(u):
+        span = pl.ds(pl.multiple_of(u * width, width), width)
+        return (
+            pltpu.make_async_copy(
+                query_w.at[span, :], weight.at[span, pl.ds(0, columns)], weight_sem.at[0, u]
+            ),
+            pltpu.make_async_copy(
+                value_w.at[span, :], weight.at[span, pl.ds(columns, HEAD)], weight_sem.at[1, u]
+            ),
+            pltpu.make_async_copy(
+                key_w.at[span, :], weight.at[span, pl.ds(columns + HEAD, HEAD)], weight_sem.at[2, u]
+            ),
+        )
+
+    def wide_copy(u):
+        span = pl.ds(pl.multiple_of(u * width, width), width)
+        return pltpu.make_async_copy(out_w.at[:, span], wide_out.at[u], wide_sem.at[u])
+
+    small = [pltpu.make_async_copy(down_hbm, down, small_sem.at[0])]
+    for a in range(owned):
+        small.append(
+            pltpu.make_async_copy(
+                up_query_hbm.at[a],
+                up.at[a, pl.ds(0, HEAD // 2), pl.ds(0, columns)],
+                small_sem.at[1 + a],
+            )
+        )
+        small.append(
+            pltpu.make_async_copy(
+                up_value_hbm.at[a],
+                up.at[a, pl.ds(HEAD // 2, HEAD // 2), pl.ds(columns, HEAD)],
+                small_sem.at[1 + owned + a],
+            )
+        )
+    order = [me, sibling]
+    for k in range(1, chips):
+        order += [at_chip(k) * CORES + core, at_chip(k) * CORES + (1 - core)]
+    for copy in weight_copies(me):
+        copy.start()
+    for copy in small:
+        copy.start()
+    for u in order[1:]:
+        for copy in weight_copies(u):
+            copy.start()
+    cache_copy = pltpu.make_async_copy(cache_hbm, cache, cache_sem)
+    cache_copy.start()
+    wide_order = []
+    for k in list(range(1, chips)) + [0]:
+        wide_order += [at_chip(k) * CORES + (1 - core), at_chip(k) * CORES + core]
+    for u in wide_order:
+        wide_copy(u).start()
+
+    barrier = pltpu.get_barrier_semaphore()
+    for k in range(1, T):
+        pl.semaphore_signal(
+            barrier, inc=1, device_id=tp(lax.rem(me + k, T)), device_id_type=MESH
+        )
+    pl.semaphore_signal(barrier, inc=1, device_id=peer, device_id_type=MESH)
+
+    token = jnp.concatenate([tokens_ref[s].astype(F32) for s in range(STEPS)], axis=0)
+    xs[side] = (token * gain_ref[...].astype(F32)).astype(BF16)
+    square = jnp.sum(token * token, axis=1, keepdims=True)
+    eye = iota((rows, HEAD), 0) == iota((rows, HEAD), 1)
+    squares[me] = jnp.broadcast_to(
+        jnp.sum(jnp.where(eye, square, 0.0), axis=0, keepdims=True), (8, HEAD)
+    )
+    request = lax.rem(iota((rows, requests), 0), requests)
+    entry = jnp.sum(
+        jnp.where(request == iota((rows, requests), 1), entry_ref[...], 0), axis=1, keepdims=True
+    )
+    slot = jnp.zeros((rows, 1), jnp.int32)
+    for n in range(need):
+        slot = jnp.where(entry == n, table_ref[ids_ref[side, n]], slot)
+    masks[side] = jnp.where(slot == iota((rows, HEAD), 1), 1.0, 0.0).astype(BF16)
+
+    pl.semaphore_wait(barrier, T)
+    sends = []
+
+    def send(copy):
+        copy.start()
+        sends.append(copy)
+
+    mine = xs.at[side]
+    send(remote(mine, gathered.at[me], x_send.at[0], x_recv.at[me], tp(sibling)))
+    send(remote(mine, xs.at[side], peer_send.at[0], peer_recv.at[0], peer))
+    send(remote(masks.at[side], masks.at[side], peer_send.at[1], peer_recv.at[1], peer))
+    for k in range(1, chips):
+        send(
+            remote(
+                mine, gathered.at[me], x_send.at[k], x_recv.at[me], tp(at_chip(k) * CORES + core)
+            )
+        )
+    for k in range(1, T):
+        send(
+            remote(
+                squares.at[me],
+                squares.at[me],
+                square_send.at[k],
+                square_recv.at[me],
+                tp(lax.rem(me + k, T)),
+            )
+        )
+
+    for a in range(owned):
+        up[a, pl.ds(HEAD // 2, HEAD // 2), pl.ds(0, columns)] = jnp.zeros(
+            (HEAD // 2, columns), BF16
+        )
+        up[a, pl.ds(0, HEAD // 2), pl.ds(columns, HEAD)] = jnp.zeros((HEAD // 2, HEAD), BF16)
+
+    def project(u, x):
+        for copy in weight_copies(u):
+            copy.wait()
+        return dot(x, weight[pl.ds(pl.multiple_of(u * width, width), width), :])
+
+    acc[...] = project(me, xs[side])
+    for copy in small:
+        copy.wait()
+
+    def mask_of(side_rows, a):
+        lane = iota((rows, HEAD), 1)
+        picked = jnp.where(lane == side * owned + a, masks[side_rows].astype(F32), 0.0)
+        return jnp.sum(picked, axis=1, keepdims=True)
+
+    def shrink(side_rows):
+        x = xs[side_rows]
+        total = jnp.zeros((rows, HEAD), F32)
+        for a in range(owned):
+            total = total + dot(x, down[a]) * mask_of(side_rows, a)
+        half_send[side_rows] = total.astype(BF16)
+
+    def wait_x(u):
+        remote(mine, gathered.at[u], x_send.at[0], x_recv.at[u], tp(sibling)).wait_recv()
+
+    shrink(side)
+    wait_x(sibling)
+    acc[...] += project(sibling, gathered[sibling])
+
+    remote(mine, xs.at[other], peer_send.at[0], peer_recv.at[0], peer).wait_recv()
+    remote(
+        masks.at[side], masks.at[other], peer_send.at[1], peer_recv.at[1], peer
+    ).wait_recv()
+    shrink(other)
+    half = remote(
+        half_send.at[1 - core], half_recv, half_sem.at[0], half_sem.at[1], tp(sibling)
+    )
+    send(half)
+
+    def take(k):
+        u = at_chip(k) * CORES + core
+        wait_x(u)
+        send(
+            remote(
+                gathered.at[u], gathered.at[u], forward_send.at[k], x_recv.at[u], tp(sibling)
+            )
+        )
+        acc[...] += project(u, gathered[u])
+
+    def take_other(k):
+        u = at_chip(k) * CORES + (1 - core)
+        wait_x(u)
+        acc[...] += project(u, gathered[u])
+
+    take(1)
+    half.wait_recv()
+    chip_total = half_send[core].astype(F32) + half_recv[...].astype(F32)
+    chip_sum[z] = chip_total.astype(BF16)
+    for k in range(1, chips):
+        send(
+            remote(
+                chip_sum.at[z],
+                chip_sum.at[z],
+                chip_send.at[k],
+                chip_recv.at[z],
+                tp(at_chip(k) * CORES + core),
+            )
+        )
+    take_other(1)
+    cache_copy.wait()
+    for j in range(here):
+        pairs[j] = cache[j].reshape(pairs.shape[1], pairs.shape[2])
+    for k in range(1, chips):
+        u = at_chip(k)
+        remote(
+            chip_sum.at[z], chip_sum.at[u], chip_send.at[0], chip_recv.at[u], tp(sibling)
+        ).wait_recv()
+        chip_total = chip_total + chip_sum[u].astype(F32)
+    ranks[core] = chip_total.astype(BF16)
+    rank_copy = remote(
+        ranks.at[core], ranks.at[core], rank_sem.at[0], rank_sem.at[1], tp(sibling)
+    )
+    send(rank_copy)
+    take(2)
+    remote(
+        ranks.at[core], ranks.at[1 - core], rank_sem.at[0], rank_sem.at[1], tp(sibling)
+    ).wait_recv()
+
+    def lift(side_rows):
+        rank = ranks[side_rows].astype(F32)
+        total = jnp.zeros((rows, columns + HEAD), F32)
+        for a in range(owned):
+            total = total + dot((rank * mask_of(side_rows, a)).astype(BF16), up[a])
+        return total
+
+    lift_send[...] = lift(other).astype(BF16)
+    lift_copy = remote(lift_send, lift_recv, lift_sem.at[0], lift_sem.at[1], peer)
+    send(lift_copy)
+    lift_own[...] = lift(side)
+    take_other(2)
+    for k in range(3, chips):
+        take(k)
+        take_other(k)
+    total_square = squares[me]
+    for k in range(1, T):
+        u = lax.rem(me + k, T)
+        remote(
+            squares.at[me], squares.at[u], square_send.at[0], square_recv.at[u], tp(sibling)
+        ).wait_recv()
+        total_square = total_square + squares[u]
+    total_column = jnp.sum(
+        jnp.where(eye, jnp.broadcast_to(total_square[0:1], (rows, HEAD)), 0.0),
+        axis=1,
+        keepdims=True,
+    )
+    factor = lax.rsqrt(total_column / (T * width) + 1e-05)
+    lift_copy.wait_recv()
+    lifted = lift_own[...] + lift_recv[...].astype(F32)
+    span = columns + HEAD
+    front = ((acc[:, 0:span] + lifted) * factor).astype(BF16)
+    last = (acc[:, span:] * factor).astype(BF16)
+
+    def spread(shape, row_axis, col_axis):
+        row = iota(shape, row_axis)
+        u = row // pad
+        i = lax.rem(row, pad)
+        step = i // here
+        source = step * requests + u * here + lax.rem(i, here)
+        return jnp.where(
+            (i < STEPS * here) & (iota(shape, col_axis) == source), 1.0, 0.0
+        ).astype(BF16)
+
+    place = spread((T * pad, rows), 0, 1)
+    heads_send[:, :, 0:span] = dot(place, front).astype(BF16).reshape(T, pad, span)
+    heads_send[:, :, span:] = dot(place, last).astype(BF16).reshape(T, pad, HEAD)
+    for k in range(1, T):
+        u = lax.rem(me + k, T)
+        send(
+            remote(
+                heads_send.at[u], heads_recv.at[me], heads_ssem.at[k], heads_rsem.at[me], tp(u)
+            )
+        )
+    heads_recv[me] = heads_send[me]
+
+    row = iota((pad, HEAD), 0)
+    lane = iota((pad, HEAD), 1)
+    step = row // here
+    index = lax.rem(row, here)
+    position = jnp.zeros((pad, HEAD), jnp.int32)
+    for j in range(here):
+        position = jnp.where(index == j, length_ref[j], position)
+    position = (position + step).astype(F32)
+    freq = jnp.exp(
+        -(lax.rem(lane, HEAD // 2).astype(F32) * 2.0 / HEAD) * math.log(500000.0)
+    )
+    angle = position * freq
+    cosine = jnp.cos(angle)
+    sine = jnp.where(lane < HEAD // 2, -jnp.sin(angle), jnp.sin(angle))
+
+    def turn(block):
+        wide = block.astype(F32)
+        return (wide * cosine + pltpu.roll(wide, HEAD // 2, 1) * sine).astype(BF16).astype(F32)
+
+    results[...] = jnp.zeros(results.shape, F32)
+    for k in range(1, T):
+        u = lax.rem(me + k, T)
+        remote(
+            heads_send.at[u], heads_recv.at[u], heads_ssem.at[0], heads_rsem.at[u], tp(sibling)
+        ).wait_recv()
+    new_keys = []
+    new_values = []
+    for h in range(T):
+        for g in range(group):
+            turned[h, pl.ds(g * pad, pad), :] = turn(
+                heads_recv[h, :, g * HEAD : (g + 1) * HEAD]
+            )
+        new_values.append(heads_recv[h, :, columns : columns + HEAD].astype(F32))
+        new_keys.append(turn(heads_recv[h, :, columns + HEAD :]))
+
+    scale = HEAD ** (-0.5)
+    per = STEPS * group
+    count = pairs.shape[1]
+    for j in range(here):
+        queries = []
+        scores = []
+        fresh = [[] for _ in range(STEPS)]
+        for h in range(T):
+            query = jnp.concatenate(
+                [
+                    turned[h, pl.ds(s * here + j, group, stride=pad), :]
+                    for s in range(STEPS)
+                ],
+                axis=0,
+            )
+            keys = pairs[j, :, h * HEAD : (h + 1) * HEAD]
+            scores.append(
+                lax.dot_general(
+                    query.astype(BF16),
+                    keys,
+                    (((1,), (1,)), ((), ())),
+                    preferred_element_type=F32,
+                )
+            )
+            for s in range(STEPS):
+                at = s * here + j
+                fresh[s].append(
+                    jnp.sum(query * new_keys[h][at : at + 1, :], axis=1, keepdims=True)
+                )
+        score = jnp.concatenate(scores, axis=0) * scale
+        lanes = iota((T * per, count), 1)
+        valid = (lanes < 2 * length_ref[j]) & (lax.rem(lanes, 2) == 0)
+        score = jnp.where(valid, score, -1e30)
+        top = jnp.max(score, axis=1, keepdims=True)
+        row_step = lax.rem(iota((T * per, 1), 0), per) // group
+        new_scores = []
+        for s in range(STEPS):
+            new = jnp.concatenate(fresh[s], axis=0) * scale
+            new = jnp.where(row_step >= s, new, -1e30)
+            new_scores.append(new)
+            top = jnp.maximum(top, new)
+        old_exp = jnp.exp(score - top)
+        total = jnp.sum(old_exp, axis=1, keepdims=True)
+        new_exp = [jnp.exp(new - top) for new in new_scores]
+        for new in new_exp:
+            total = total + new
+        inverse = 1.0 / total
+        shifted = pltpu.roll(old_exp * inverse, 1, 1).astype(BF16)
+        new_weight = [(new * inverse).astype(BF16).astype(F32) for new in new_exp]
+        for h in range(T):
+            part = slice(h * per, (h + 1) * per)
+            result = dot(shifted[part], pairs[j, :, h * HEAD : (h + 1) * HEAD])
+            for s in range(STEPS):
+                at = s * here + j
+                result = result + new_weight[s][part] * new_values[h][at : at + 1, :]
+            for s in range(STEPS):
+                results[h, pl.ds(s * here + j, group, stride=pad), :] = result[
+                    s * group : (s + 1) * group
+                ]
+    for h in range(T):
+        for g in range(group):
+            back_send[h, :, g * HEAD : (g + 1) * HEAD] = results[
+                h, pl.ds(g * pad, pad), :
+            ].astype(BF16)
+    for k in range(1, T):
+        u = lax.rem(me + k, T)
+        send(
+            remote(back_send.at[u], back_recv.at[me], back_ssem.at[k], back_rsem.at[me], tp(u))
+        )
+    back_recv[me] = back_send[me]
+    collect = spread((rows, T * pad), 1, 0)
+    for k in range(1, T):
+        u = lax.rem(me + k, T)
+        remote(
+            back_send.at[u], back_recv.at[u], back_ssem.at[0], back_rsem.at[u], tp(sibling)
+        ).wait_recv()
+    attended = dot(collect, back_recv[...].reshape(T * pad, columns)).astype(BF16)
+
+    def forward(k):
+        u = at_chip(k) * CORES + (1 - core)
+        wide_copy(u).wait()
+        sib_send[k] = dot(attended, wide_out[u]).astype(BF16)
+        send(remote(sib_send.at[k], sib_recv.at[k], sib_ssem.at[k], sib_rsem.at[k], tp(sibling)))
+        v = at_chip(k) * CORES + core
+        wide_copy(v).wait()
+        own_part[k] = dot(attended, wide_out[v])
+
+    def finish(k):
+        remote(
+            sib_send.at[k], sib_recv.at[k], sib_ssem.at[k], sib_rsem.at[k], tp(sibling)
+        ).wait_recv()
+        summed = own_part[k] + sib_recv[k].astype(F32)
+        if k == 0:
+            own_part[0] = summed
+        else:
+            sum_send[k] = summed.astype(BF16)
+            send(
+                remote(
+                    sum_send.at[k],
+                    sum_recv.at[z],
+                    sum_ssem.at[k],
+                    sum_rsem.at[z],
+                    tp(at_chip(k) * CORES + core),
+                )
+            )
+
+    turns = list(range(1, chips)) + [0]
+    for i, k in enumerate(turns):
+        forward(k)
+        if i:
+            finish(turns[i - 1])
+    finish(0)
+    mixed = token + own_part[0]
+    for k in range(1, chips):
+        u = at_chip(k)
+        remote(
+            sum_send.at[k], sum_recv.at[u], sum_ssem.at[k], sum_rsem.at[u], tp(sibling)
+        ).wait_recv()
+        mixed = mixed + sum_recv[u].astype(F32)
+    for s in range(STEPS):
+        out_ref[s] = mixed[s * requests : (s + 1) * requests].astype(BF16)
+    for copy in sends:
+        copy.wait_send()
+
+
+def fused(
+    tokens,
+    input_norm_gain,
+    query_weight,
+    key_weight,
+    value_weight,
+    output_weight,
+    adapter_down_maps,
+    adapter_query_up,
+    adapter_value_up,
+    key_value_cache,
+    cached_length,
+    request_adapter_entry,
+    group_adapter_ids,
+    adapter_slot_table,
+):
+    T = lax.axis_size("tp")
+    chips = T // CORES
+    requests = tokens.shape[1]
+    rows = STEPS * requests
+    width = tokens.shape[2]
+    here = cached_length.shape[0]
+    owned = adapter_down_maps.shape[0]
+    columns = query_weight.shape[1]
+    group = columns // HEAD
+    span = columns + HEAD
+    pad = 16
+    count = 2 * key_value_cache.shape[1]
+    sizes = (T, requests, here, owned, group_adapter_ids.shape[1])
+    whole = pl.BlockSpec(memory_space=pltpu.VMEM)
+    scalar = pl.BlockSpec(memory_space=pltpu.SMEM)
+    left = pl.BlockSpec(memory_space=pl.ANY)
+    dma = pltpu.SemaphoreType.DMA
+    vmem = pltpu.VMEM
+    return pl.pallas_call(
+        functools.partial(block_kernel, sizes),
+        out_shape=jax.ShapeDtypeStruct(tokens.shape, BF16),
+        in_specs=[whole] * 3 + [scalar] * 3 + [left] * 8,
+        out_specs=whole,
+        scratch_shapes=[
+            vmem((T * width, span + HEAD), BF16),
+            vmem((T, columns, width), BF16),
+            vmem(adapter_down_maps.shape, BF16),
+            vmem((owned, HEAD, span), BF16),
+            vmem(key_value_cache.shape, BF16),
+            vmem((here, count, KV_HEADS * HEAD), BF16),
+            vmem((T, rows, width), BF16),
+            vmem((2, rows, width), BF16),
+            vmem((2, rows, HEAD), BF16),
+            vmem((T, 8, HEAD), F32),
+            vmem((rows, span + HEAD), F32),
+            vmem((2, rows, HEAD), BF16),
+            vmem((rows, HEAD), BF16),
+            vmem((chips, rows, HEAD), BF16),
+            vmem((2, rows, HEAD), BF16),
+            vmem((rows, span), F32),
+            vmem((rows, span), BF16),
+            vmem((rows, span), BF16),
+            vmem((T, pad, span + HEAD), BF16),
+            vmem((T, pad, span + HEAD), BF16),
+            vmem((T, group * pad, HEAD), F32),
+            vmem((T, group * pad, HEAD), F32),
+            vmem((T, pad, columns), BF16),
+            vmem((T, pad, columns), BF16),
+            vmem((chips, rows, width), F32),
+            vmem((chips, rows, width), BF16),
+            vmem((chips, rows, width), BF16),
+            vmem((chips, rows, width), BF16),
+            vmem((chips, rows, width), BF16),
+            dma((3, T)),
+            dma((T,)),
+            dma((1 + 2 * owned,)),
+            dma(()),
+            dma((chips,)),
+            dma((T,)),
+            dma((chips,)),
+            dma((2,)),
+            dma((2,)),
+            dma((T,)),
+            dma((T,)),
+            dma((2,)),
+            dma((chips,)),
+            dma((chips,)),
+            dma((2,)),
+            dma((2,)),
+            dma((T,)),
+            dma((T,)),
+            dma((T,)),
+            dma((T,)),
+            dma((chips,)),
+            dma((chips,)),
+            dma((chips,)),
+            dma((chips,)),
+        ],
+        compiler_params=pltpu.CompilerParams(
+            collective_id=0, has_side_effects=True, vmem_limit_bytes=56 * 1024 * 1024
+        ),
+    )(
+        tokens,
+        input_norm_gain.reshape(1, width),
+        request_adapter_entry.reshape(1, requests),
+        group_adapter_ids,
+        adapter_slot_table,
+        cached_length,
+        query_weight,
+        key_weight,
+        value_weight,
+        output_weight,
+        adapter_down_maps,
+        adapter_query_up,
+        adapter_value_up,
+        key_value_cache,
+    )
+
+
+def device_program(*arrays):
+    tokens, query_weight, key_weight, down = arrays[0], arrays[2], arrays[3], arrays[6]
+    T = lax.axis_size("tp")
+    whole_heads = (
+        key_weight.shape[1] == HEAD
+        and T == KV_HEADS
+        and lax.axis_size("srv") == 2
+        and down.shape[2] == HEAD
+        and tokens.shape[2] == query_weight.shape[1]
+        and (STEPS * tokens.shape[1]) % 16 == 0
+        and STEPS * tokens.shape[1] <= HEAD
+    )
+    return fused(*arrays) if whole_heads else on_device(*arrays)
+
+
 def solution(mesh):
     placed = (
         P(None, ("rep", "srv"), "tp"),
@@ -188,7 +849,7 @@
         P(),
     )
     return jax.shard_map(
-        on_device,
+        device_program,
         mesh=mesh,
         in_specs=placed,
         out_specs=P(None, ("rep", "srv"), "tp"),

time: 290 us -> 74.7 us (0.26)
  waiting for transfers between devices: 85.9 us -> 0 us
  Pallas kernels: 0 us -> 70.6 us
  local copies, waits for them, and re-layouts: 70.8 us -> 2.87 us
  blocking collectives: 60.9 us -> 0 us
  matrix products: 27.1 us -> 0 us
  other arithmetic: 19.7 us -> 0 us
  between operations: 13.6 us -> 0.01 us
  starting transfers between devices: 10.3 us -> 0 us
    pallas_call x0 -> x1, Pallas kernels: none -> 70.6 us  [fused(): pl.pallas_call(functools.partial(block_kernel, sizes), out_shape=jax.Shap...]
    reduce_scatter x1 -> x0, waiting for transfers between devices: 36.9 us -> none  [on_device(): lax.psum_scatter(lax.dot_general(output_weight, flat_heads, (((0,), (1,))...]
    all_gather x3 -> x0, waiting for transfers between devices: 35.3 us -> none  [the longest x1 21.9 us: on_device(): whole = lax.all_gather(flat, 'tp', axis=1, tiled=True)]
    psum x1 -> x0, blocking collectives: 29.7 us -> none  [on_device(): rank_row_values = lax.psum(shrunk, 'tp').astype(jnp.bfloat16)]
    unnamed x28 -> x1, local copies, waits for them, and re-layouts: 29.4 us -> 1.59 us
    dot_general x14 -> x0, matrix products: 27.1 us -> none  [the longest x1 10.4 us: on_device(): lax.dot_general(output_weight, flat_heads, (((0,), (1,)), ((), ())), pref...]
    all_gather x2 -> x0, blocking collectives: 21.3 us -> none  [the longest x1 14.5 us: on_device(): gain = lax.all_gather(input_norm_gain, 'tp', axis=0, tiled=True)]
    convert_element_type x6 -> x0, local copies, waits for them, and re-layouts: 14 us -> none  [the longest x4 13.9 us: attend(): return result.reshape(rows, KV_HEADS * group * HEAD).astype(jnp.bfloat16)]
  transfers between devices with their start and end apart: 7 -> 0, of which waited for: 5 -> 0; matrix products, arithmetic and copies ran while one was open for 15% -> 0% of each run, Pallas kernels for 0% -> 0%
where the time goes in v1:
time: 74.7 us; the launch traced here: 73.5 us
  Pallas kernels  70.6 us (95%)
  local copies, waits for them, and re-layouts  2.87 us (4%)
    pallas_call x1, Pallas kernels, fused(): pl.pallas_call(functools.partial(block_kernel, sizes), out_shape=jax.Shap...  70.6 us
    unnamed x1, local copies, waits for them, and re-layouts  1.59 us

profile of v1, /device:TPU:0, one launch (start us, length us, event | category | flops | bytes accessed | tf_op | source)
XLA Modules:
  0.0 73.5 jit_solution(8209231422647384167)
XLA Ops:
  0.0 1.3 %reshape.6.gain_ref = bf16[1,1024]{1,0:T(2,128)(2,1)} reshape(bf16[1024]{0:T(1024)(128)(2,1)} %param.15) | data formatting | bytes 4096 | tf_op jit(solution)/shard_map/reshape | solution.py:803
  1.3 70.6 %shard_map.136 = bf16[2,40,1024]{2,1,0:T(8,128)(2,1)} custom-call(bf16[2,40,1024]{2,1,0:T(8,128)(2,1)} %tokens_ref.1, bf16[1,1024]{1,0:T(2,128)(2,1)} %reshape.6.gain_ref, s32[1,40]{1,0:T(1,128)} %bitcast.1, s32[2,3]{1,0:T(2,128)} %ids_ref.1, s32[8]{0:T(128)} %table_ref.1, s32[5]{0:T(128)} %length_ref.1, bf16[8192,1024]{1,0:T(8,128)(2,1)} %query_w.1, ...), custom_call_target="tpu_custom_call" | custom-call | tf_op jit(solution)/shard_map/pallas_call | solution.py:738
  71.9 1.6 %copy.16 = bf16[2,40,1024]{2,1,0:T(8,128)(2,1)} copy(bf16[2,40,1024]{2,1,0:T(8,128)(2,1)} %shard_map.136) | data formatting | bytes 327680

commit v2 on v1

--- a/solution.py
+++ b/solution.py
@@ -220,9 +220,10 @@
     cache,
     pairs,
     gathered,
-    xs,
+    raw,
     masks,
-    squares,
+    stats,
+    totals,
     acc,
     half_send,
     half_recv,
@@ -248,11 +249,12 @@
     cache_sem,
     x_send,
     x_recv,
+    line_send,
     forward_send,
     peer_send,
     peer_recv,
-    square_send,
-    square_recv,
+    stat_send,
+    stat_recv,
     half_sem,
     chip_send,
     chip_recv,
@@ -288,6 +290,29 @@
         return lax.rem(z + k, chips)
 
     peer = {"srv": other}
+    last = chips - 1
+
+    def pick(lists, i):
+        value = lists[0][i]
+        for at in range(1, chips):
+            value = jnp.where(z == at, lists[at][i], value)
+        return value
+
+    near = [
+        sorted((v for v in range(chips) if v != at), key=lambda v: (abs(v - at), v))
+        for at in range(chips)
+    ]
+
+    def ready(at, v):
+        if v == at:
+            return 4 * chips
+        return at + last - v if v > at else last - at + v
+
+    onward = [
+        sorted(range(chips), key=lambda v: (ready(at, v), abs(v - at))) for at in range(chips)
+    ]
+    sources = [pick(near, i) for i in range(last)]
+    targets = [pick(onward, i) for i in range(chips)]
 
     def weight_copies(u):
         span = pl.ds(pl.multiple_of(u * width, width), width)
@@ -324,20 +349,20 @@
             )
         )
     order = [me, sibling]
-    for k in range(1, chips):
-        order += [at_chip(k) * CORES + core, at_chip(k) * CORES + (1 - core)]
+    for v in sources:
+        order += [v * CORES + core, v * CORES + (1 - core)]
     for copy in weight_copies(me):
         copy.start()
     for copy in small:
         copy.start()
+    cache_copy = pltpu.make_async_copy(cache_hbm, cache, cache_sem)
+    cache_copy.start()
     for u in order[1:]:
         for copy in weight_copies(u):
             copy.start()
-    cache_copy = pltpu.make_async_copy(cache_hbm, cache, cache_sem)
-    cache_copy.start()
     wide_order = []
-    for k in list(range(1, chips)) + [0]:
-        wide_order += [at_chip(k) * CORES + (1 - core), at_chip(k) * CORES + core]
+    for v in targets:
+        wide_order += [v * CORES + (1 - core), v * CORES + core]
     for u in wide_order:
         wide_copy(u).start()
 
@@ -349,12 +374,20 @@
     pl.semaphore_signal(barrier, inc=1, device_id=peer, device_id_type=MESH)
 
     token = jnp.concatenate([tokens_ref[s].astype(F32) for s in range(STEPS)], axis=0)
-    xs[side] = (token * gain_ref[...].astype(F32)).astype(BF16)
+    raw[side] = token.astype(BF16)
     square = jnp.sum(token * token, axis=1, keepdims=True)
     eye = iota((rows, HEAD), 0) == iota((rows, HEAD), 1)
-    squares[me] = jnp.broadcast_to(
-        jnp.sum(jnp.where(eye, square, 0.0), axis=0, keepdims=True), (8, HEAD)
-    )
+    square = jnp.sum(jnp.where(eye, square, 0.0), axis=0, keepdims=True)
+    high = square.astype(BF16).astype(F32)
+    middle = (square - high).astype(BF16).astype(F32)
+    low = square - high - middle
+    gain = gain_ref[...].astype(F32)
+    gain_rows = width // HEAD
+    stats[me] = jnp.concatenate(
+        [gain[:, i * HEAD : (i + 1) * HEAD] for i in range(gain_rows)]
+        + [high, middle, low, jnp.zeros((16 - 3 - gain_rows, HEAD), F32)],
+        axis=0,
+    ).astype(BF16)
     request = lax.rem(iota((rows, requests), 0), requests)
     entry = jnp.sum(
         jnp.where(request == iota((rows, requests), 1), entry_ref[...], 0), axis=1, keepdims=True
@@ -371,26 +404,36 @@
         copy.start()
         sends.append(copy)
 
-    mine = xs.at[side]
-    send(remote(mine, gathered.at[me], x_send.at[0], x_recv.at[me], tp(sibling)))
-    send(remote(mine, xs.at[side], peer_send.at[0], peer_recv.at[0], peer))
-    send(remote(masks.at[side], masks.at[side], peer_send.at[1], peer_recv.at[1], peer))
-    for k in range(1, chips):
-        send(
-            remote(
-                mine, gathered.at[me], x_send.at[k], x_recv.at[me], tp(at_chip(k) * CORES + core)
-            )
-        )
+    mine = raw.at[side]
     for k in range(1, T):
         send(
             remote(
-                squares.at[me],
-                squares.at[me],
-                square_send.at[k],
-                square_recv.at[me],
-                tp(lax.rem(me + k, T)),
-            )
-        )
+                stats.at[me], stats.at[me], stat_send.at[k], stat_recv.at[me], tp(lax.rem(me + k, T))
+            )
+        )
+
+    def conditional(condition, copy):
+        @pl.when(condition)
+        def _():
+            copy.start()
+
+        maybe.append((condition, copy))
+
+    maybe = []
+
+    def along(u, block, right, left, i):
+        for condition, step, s in ((right, 1, 0), (left, -1, 1)):
+            conditional(
+                condition,
+                remote(
+                    block, gathered.at[u], line_send.at[i, s], x_recv.at[u], tp(me + step * CORES)
+                ),
+            )
+
+    along(me, mine, z < last, z > 0, 0)
+    send(remote(masks.at[side], masks.at[side], peer_send.at[1], peer_recv.at[1], peer))
+    send(remote(mine, raw.at[side], peer_send.at[0], peer_recv.at[0], peer))
+    send(remote(mine, gathered.at[me], x_send, x_recv.at[me], tp(sibling)))
 
     for a in range(owned):
         up[a, pl.ds(HEAD // 2, HEAD // 2), pl.ds(0, columns)] = jnp.zeros(
@@ -403,7 +446,45 @@
             copy.wait()
         return dot(x, weight[pl.ds(pl.multiple_of(u * width, width), width), :])
 
-    acc[...] = project(me, xs[side])
+    cache_copy.wait()
+    for j in range(here):
+        pairs[j] = cache[j].reshape(pairs.shape[1], pairs.shape[2])
+
+    def squares_of(u):
+        block = stats[u].astype(F32)
+        top_row = gain_rows
+        return (
+            block[top_row : top_row + 1]
+            + block[top_row + 1 : top_row + 2]
+            + block[top_row + 2 : top_row + 3]
+        )
+
+    def gain_of(u):
+        block = stats[u].astype(F32)
+        return jnp.concatenate([block[i : i + 1] for i in range(gain_rows)], axis=1)
+
+    def factor_of(total):
+        column = jnp.sum(
+            jnp.where(eye, jnp.broadcast_to(total, (rows, HEAD)), 0.0), axis=1, keepdims=True
+        )
+        return lax.rsqrt(column / (T * width) + 1e-05)
+
+    total_square = squares_of(me)
+    for k in range(1, T):
+        u = lax.rem(me + k, T)
+        remote(
+            stats.at[me], stats.at[u], stat_send.at[0], stat_recv.at[u], tp(sibling)
+        ).wait_recv()
+        total_square = total_square + squares_of(u)
+    totals[side] = jnp.broadcast_to(total_square, (8, HEAD))
+    send(remote(totals.at[side], totals.at[side], peer_send.at[2], peer_recv.at[2], peer))
+    factor = factor_of(total_square)
+
+    def normed(block, row_factor, u):
+        return (block.astype(F32) * row_factor * gain_of(u)).astype(BF16)
+
+    normed_mine = normed(raw[side], factor, me)
+    acc[...] = project(me, normed_mine)
     for copy in small:
         copy.wait()
 
@@ -412,49 +493,50 @@
         picked = jnp.where(lane == side * owned + a, masks[side_rows].astype(F32), 0.0)
         return jnp.sum(picked, axis=1, keepdims=True)
 
-    def shrink(side_rows):
-        x = xs[side_rows]
+    def shrink(side_rows, x):
         total = jnp.zeros((rows, HEAD), F32)
         for a in range(owned):
             total = total + dot(x, down[a]) * mask_of(side_rows, a)
-        half_send[side_rows] = total.astype(BF16)
+        half_send[side_rows] = total
 
     def wait_x(u):
-        remote(mine, gathered.at[u], x_send.at[0], x_recv.at[u], tp(sibling)).wait_recv()
-
-    shrink(side)
-    wait_x(sibling)
-    acc[...] += project(sibling, gathered[sibling])
-
-    remote(mine, xs.at[other], peer_send.at[0], peer_recv.at[0], peer).wait_recv()
-    remote(
-        masks.at[side], masks.at[other], peer_send.at[1], peer_recv.at[1], peer
-    ).wait_recv()
-    shrink(other)
+        remote(mine, gathered.at[u], x_send, x_recv.at[u], tp(sibling)).wait_recv()
+
+    def add_block(u):
+        acc[...] += project(u, normed(gathered[u], factor, u))
+
+    def arrive(i):
+        v = sources[i]
+        u = v * CORES + core
+        wait_x(u)
+        along(u, gathered.at[u], (v < z) & (z < last), (v > z) & (z > 0), i + 1)
+        send(
+            remote(gathered.at[u], gathered.at[u], forward_send.at[i], x_recv.at[u], tp(sibling))
+        )
+
+    def add_same(i):
+        add_block(sources[i] * CORES + core)
+
+    def add_other(i):
+        u = sources[i] * CORES + (1 - core)
+        wait_x(u)
+        add_block(u)
+
+    shrink(side, normed_mine)
+    arrive(0)
+    remote(masks.at[side], masks.at[other], peer_send.at[1], peer_recv.at[1], peer).wait_recv()
+    remote(totals.at[side], totals.at[other], peer_send.at[2], peer_recv.at[2], peer).wait_recv()
+    remote(mine, raw.at[other], peer_send.at[0], peer_recv.at[0], peer).wait_recv()
+    shrink(other, normed(raw[other], factor_of(totals[other][0:1]), me))
     half = remote(
         half_send.at[1 - core], half_recv, half_sem.at[0], half_sem.at[1], tp(sibling)
     )
     send(half)
-
-    def take(k):
-        u = at_chip(k) * CORES + core
-        wait_x(u)
-        send(
-            remote(
-                gathered.at[u], gathered.at[u], forward_send.at[k], x_recv.at[u], tp(sibling)
-            )
-        )
-        acc[...] += project(u, gathered[u])
-
-    def take_other(k):
-        u = at_chip(k) * CORES + (1 - core)
-        wait_x(u)
-        acc[...] += project(u, gathered[u])
-
-    take(1)
+    wait_x(sibling)
+    add_block(sibling)
     half.wait_recv()
-    chip_total = half_send[core].astype(F32) + half_recv[...].astype(F32)
-    chip_sum[z] = chip_total.astype(BF16)
+    chip_total = half_send[core] + half_recv[...]
+    chip_sum[z] = chip_total.astype(chip_sum.dtype)
     for k in range(1, chips):
         send(
             remote(
@@ -465,22 +547,22 @@
                 tp(at_chip(k) * CORES + core),
             )
         )
-    take_other(1)
-    cache_copy.wait()
-    for j in range(here):
-        pairs[j] = cache[j].reshape(pairs.shape[1], pairs.shape[2])
+    add_same(0)
+    arrive(1)
+    add_other(0)
+    add_same(1)
     for k in range(1, chips):
-        u = at_chip(k)
+        v = at_chip(k)
         remote(
-            chip_sum.at[z], chip_sum.at[u], chip_send.at[0], chip_recv.at[u], tp(sibling)
+            chip_sum.at[z], chip_sum.at[v], chip_send.at[0], chip_recv.at[v], tp(sibling)
         ).wait_recv()
-        chip_total = chip_total + chip_sum[u].astype(F32)
+        chip_total = chip_total + chip_sum[v].astype(F32)
     ranks[core] = chip_total.astype(BF16)
     rank_copy = remote(
         ranks.at[core], ranks.at[core], rank_sem.at[0], rank_sem.at[1], tp(sibling)
     )
     send(rank_copy)
-    take(2)
+    add_other(1)
     remote(
         ranks.at[core], ranks.at[1 - core], rank_sem.at[0], rank_sem.at[1], tp(sibling)
     ).wait_recv()
@@ -496,28 +578,14 @@
     lift_copy = remote(lift_send, lift_recv, lift_sem.at[0], lift_sem.at[1], peer)
     send(lift_copy)
     lift_own[...] = lift(side)
-    take_other(2)
-    for k in range(3, chips):
-        take(k)
-        take_other(k)
-    total_square = squares[me]
-    for k in range(1, T):
-        u = lax.rem(me + k, T)
-        remote(
-            squares.at[me], squares.at[u], square_send.at[0], square_recv.at[u], tp(sibling)
-        ).wait_recv()
-        total_square = total_square + squares[u]
-    total_column = jnp.sum(
-        jnp.where(eye, jnp.broadcast_to(total_square[0:1], (rows, HEAD)), 0.0),
-        axis=1,
-        keepdims=True,
-    )
-    factor = lax.rsqrt(total_column / (T * width) + 1e-05)
+    for i in range(2, last):
+        arrive(i)
+        add_same(i)
+        add_other(i)
     lift_copy.wait_recv()
-    lifted = lift_own[...] + lift_recv[...].astype(F32)
     span = columns + HEAD
-    front = ((acc[:, 0:span] + lifted) * factor).astype(BF16)
-    last = (acc[:, span:] * factor).astype(BF16)
+    front = (acc[:, 0:span] + lift_own[...] + lift_recv[...].astype(F32)).astype(BF16)
+    key_block = acc[:, span:].astype(BF16)
 
     def spread(shape, row_axis, col_axis):
         row = iota(shape, row_axis)
@@ -531,7 +599,7 @@
 
     place = spread((T * pad, rows), 0, 1)
     heads_send[:, :, 0:span] = dot(place, front).astype(BF16).reshape(T, pad, span)
-    heads_send[:, :, span:] = dot(place, last).astype(BF16).reshape(T, pad, HEAD)
+    heads_send[:, :, span:] = dot(place, key_block).astype(BF16).reshape(T, pad, HEAD)
     for k in range(1, T):
         u = lax.rem(me + k, T)
         send(
@@ -654,51 +722,79 @@
         ).wait_recv()
     attended = dot(collect, back_recv[...].reshape(T * pad, columns)).astype(BF16)
 
-    def forward(k):
-        u = at_chip(k) * CORES + (1 - core)
-        wide_copy(u).wait()
-        sib_send[k] = dot(attended, wide_out[u]).astype(BF16)
-        send(remote(sib_send.at[k], sib_recv.at[k], sib_ssem.at[k], sib_rsem.at[k], tp(sibling)))
-        v = at_chip(k) * CORES + core
-        wide_copy(v).wait()
-        own_part[k] = dot(attended, wide_out[v])
-
-    def finish(k):
+    parts = own_part.shape[1]
+    piece = width // parts
+
+    def multiply(i, p):
+        lanes = pl.ds(p * piece, piece)
+        u = targets[i] * CORES + (1 - core)
+        v = targets[i] * CORES + core
+        if p == 0:
+            wide_copy(u).wait()
+            wide_copy(v).wait()
+        sib_send[i, p] = dot(attended, wide_out[u, :, lanes]).astype(BF16)
+        send(
+            remote(
+                sib_send.at[i, p],
+                sib_recv.at[i, p],
+                sib_ssem.at[i, p],
+                sib_rsem.at[i, p],
+                tp(sibling),
+            )
+        )
+        own_part[i, p] = dot(attended, wide_out[v, :, lanes])
+
+    def take(i, v, p, way, condition):
+        @pl.when(condition)
+        def _():
+            remote(
+                sum_send.at[i, p],
+                sum_recv.at[way, v, p],
+                sum_ssem.at[i, p],
+                sum_rsem.at[way, v, p],
+                tp(sibling),
+            ).wait_recv()
+            own_part[i, p] += sum_recv[way, v, p].astype(F32)
+
+    def finish(i, p):
         remote(
-            sib_send.at[k], sib_recv.at[k], sib_ssem.at[k], sib_rsem.at[k], tp(sibling)
+            sib_send.at[i, p], sib_recv.at[i, p], sib_ssem.at[i, p], sib_rsem.at[i, p], tp(sibling)
         ).wait_recv()
-        summed = own_part[k] + sib_recv[k].astype(F32)
-        if k == 0:
-            own_part[0] = summed
-        else:
-            sum_send[k] = summed.astype(BF16)
-            send(
-                remote(
-                    sum_send.at[k],
-                    sum_recv.at[z],
-                    sum_ssem.at[k],
-                    sum_rsem.at[z],
-                    tp(at_chip(k) * CORES + core),
-                )
-            )
-
-    turns = list(range(1, chips)) + [0]
-    for i, k in enumerate(turns):
-        forward(k)
-        if i:
-            finish(turns[i - 1])
-    finish(0)
-    mixed = token + own_part[0]
-    for k in range(1, chips):
-        u = at_chip(k)
-        remote(
-            sum_send.at[k], sum_recv.at[u], sum_ssem.at[k], sum_rsem.at[u], tp(sibling)
-        ).wait_recv()
-        mixed = mixed + sum_recv[u].astype(F32)
+        own_part[i, p] += sib_recv[i, p].astype(F32)
+        v = targets[i]
+        if i == last:
+            take(i, v, p, 0, z > 0)
+            take(i, v, p, 1, z < last)
+            return
+        take(i, v, p, 0, (v > z) & (z > 0))
+        take(i, v, p, 1, (v < z) & (z < last))
+        sum_send[i, p] = own_part[i, p].astype(BF16)
+        way = jnp.where(v > z, 0, 1)
+        send(
+            remote(
+                sum_send.at[i, p],
+                sum_recv.at[way, v, p],
+                sum_ssem.at[i, p],
+                sum_rsem.at[way, v, p],
+                tp(me + jnp.where(v > z, CORES, -CORES)),
+            )
+        )
+
+    items = [(i, p) for i in range(chips) for p in range(parts)]
+    ahead = 2
+    for item in items[:ahead]:
+        multiply(*item)
+    for n, item in enumerate(items):
+        if n + ahead < len(items):
+            multiply(*items[n + ahead])
+        finish(*item)
+    mixed = token + jnp.concatenate([own_part[last, p] for p in range(parts)], axis=1)
     for s in range(STEPS):
         out_ref[s] = mixed[s * requests : (s + 1) * requests].astype(BF16)
     for copy in sends:
         copy.wait_send()
+    for condition, copy in maybe:
+        pl.when(condition)(copy.wait_send)
 
 
 def fused(
@@ -750,11 +846,12 @@
             vmem((T, rows, width), BF16),
             vmem((2, rows, width), BF16),
             vmem((2, rows, HEAD), BF16),
-            vmem((T, 8, HEAD), F32),
+            vmem((T, 16, HEAD), BF16),
+            vmem((2, 8, HEAD), F32),
             vmem((rows, span + HEAD), F32),
-            vmem((2, rows, HEAD), BF16),
-            vmem((rows, HEAD), BF16),
-            vmem((chips, rows, HEAD), BF16),
+            vmem((2, rows, HEAD), F32),
+            vmem((rows, HEAD), F32),
+            vmem((chips, rows, HEAD), F32),
             vmem((2, rows, HEAD), BF16),
             vmem((rows, span), F32),
             vmem((rows, span), BF16),
@@ -765,20 +862,21 @@
             vmem((T, group * pad, HEAD), F32),
             vmem((T, pad, columns), BF16),
             vmem((T, pad, columns), BF16),
-            vmem((chips, rows, width), F32),
-            vmem((chips, rows, width), BF16),
-            vmem((chips, rows, width), BF16),
-            vmem((chips, rows, width), BF16),
-            vmem((chips, rows, width), BF16),
+            vmem((chips, 2, rows, width // 2), F32),
+            vmem((chips, 2, rows, width // 2), BF16),
+            vmem((chips, 2, rows, width // 2), BF16),
+            vmem((chips, 2, rows, width // 2), BF16),
+            vmem((2, chips, 2, rows, width // 2), BF16),
             dma((3, T)),
             dma((T,)),
             dma((1 + 2 * owned,)),
             dma(()),
+            dma(()),
+            dma((T,)),
+            dma((chips, 2)),
             dma((chips,)),
-            dma((T,)),
-            dma((chips,)),
-            dma((2,)),
-            dma((2,)),
+            dma((3,)),
+            dma((3,)),
             dma((T,)),
             dma((T,)),
             dma((2,)),
@@ -790,10 +888,10 @@
             dma((T,)),
             dma((T,)),
             dma((T,)),
-            dma((chips,)),
-            dma((chips,)),
-            dma((chips,)),
-            dma((chips,)),
+            dma((chips, 2)),
+            dma((chips, 2)),
+            dma((chips, 2)),
+            dma((2, chips, 2)),
         ],
         compiler_params=pltpu.CompilerParams(
             collective_id=0, has_side_effects=True, vmem_limit_bytes=56 * 1024 * 1024
@@ -825,6 +923,7 @@
         and lax.axis_size("srv") == 2
         and down.shape[2] == HEAD
         and tokens.shape[2] == query_weight.shape[1]
+        and tokens.shape[2] <= 13 * HEAD
         and (STEPS * tokens.shape[1]) % 16 == 0
         and STEPS * tokens.shape[1] <= HEAD
     )

time: 74.7 us -> 73.7 us (0.987); the launches traced: 73.5 us -> 73.5 us
  no operation moved by 1% of the time
where the time goes in v2:
time: 73.7 us; the launch traced here: 73.5 us
  Pallas kernels  70.6 us (96%)
  local copies, waits for them, and re-layouts  2.87 us (4%)
    pallas_call x1, Pallas kernels, fused(): pl.pallas_call(functools.partial(block_kernel, sizes), out_shape=jax.Shap...  70.6 us
    unnamed x1, local copies, waits for them, and re-layouts  1.59 us

profile of v2, /device:TPU:0, one launch (start us, length us, event | category | flops | bytes accessed | tf_op | source)
XLA Modules:
  0.0 73.5 jit_solution(7426513195929345042)
XLA Ops:
  0.0 1.3 %reshape.6.gain_ref = bf16[1,1024]{1,0:T(2,128)(2,1)} reshape(bf16[1024]{0:T(1024)(128)(2,1)} %param.15) | data formatting | bytes 4096 | tf_op jit(solution)/shard_map/reshape | solution.py:901
  1.3 70.6 %shard_map.136 = bf16[2,40,1024]{2,1,0:T(8,128)(2,1)} custom-call(bf16[2,40,1024]{2,1,0:T(8,128)(2,1)} %tokens_ref.1, bf16[1,1024]{1,0:T(2,128)(2,1)} %reshape.6.gain_ref, s32[1,40]{1,0:T(1,128)} %bitcast.1, s32[2,3]{1,0:T(2,128)} %ids_ref.1, s32[8]{0:T(128)} %table_ref.1, s32[5]{0:T(128)} %length_ref.1, bf16[8192,1024]{1,0:T(8,128)(2,1)} %query_w.1, ...), custom_call_target="tpu_custom_call" | custom-call | tf_op jit(solution)/shard_map/pallas_call | solution.py:834
  71.9 1.6 %copy.16 = bf16[2,40,1024]{2,1,0:T(8,128)(2,1)} copy(bf16[2,40,1024]{2,1,0:T(8,128)(2,1)} %shard_map.136) | data formatting | bytes 327680

commit v3 on v2

--- a/solution.py
+++ b/solution.py
@@ -356,15 +356,18 @@
     for copy in small:
         copy.start()
     cache_copy = pltpu.make_async_copy(cache_hbm, cache, cache_sem)
-    cache_copy.start()
-    for u in order[1:]:
-        for copy in weight_copies(u):
-            copy.start()
     wide_order = []
     for v in targets:
         wide_order += [v * CORES + (1 - core), v * CORES + core]
-    for u in wide_order:
-        wide_copy(u).start()
+
+    early = 3
+    begun = [1]
+
+    def begin(upto):
+        for u in order[begun[0] : upto]:
+            for copy in weight_copies(u):
+                copy.start()
+        begun[0] = max(begun[0], upto)
 
     barrier = pltpu.get_barrier_semaphore()
     for k in range(1, T):
@@ -405,6 +408,8 @@
         sends.append(copy)
 
     mine = raw.at[side]
+    send(remote(masks.at[side], masks.at[side], peer_send.at[1], peer_recv.at[1], peer))
+    send(remote(mine, raw.at[side], peer_send.at[0], peer_recv.at[0], peer))
     for k in range(1, T):
         send(
             remote(
@@ -431,9 +436,8 @@
             )
 
     along(me, mine, z < last, z > 0, 0)
-    send(remote(masks.at[side], masks.at[side], peer_send.at[1], peer_recv.at[1], peer))
-    send(remote(mine, raw.at[side], peer_send.at[0], peer_recv.at[0], peer))
     send(remote(mine, gathered.at[me], x_send, x_recv.at[me], tp(sibling)))
+    begin(early)
 
     for a in range(owned):
         up[a, pl.ds(HEAD // 2, HEAD // 2), pl.ds(0, columns)] = jnp.zeros(
@@ -441,14 +445,32 @@
         )
         up[a, pl.ds(0, HEAD // 2), pl.ds(columns, HEAD)] = jnp.zeros((HEAD // 2, HEAD), BF16)
 
+    used = [0]
+
     def project(u, x):
         for copy in weight_copies(u):
             copy.wait()
+        used[0] += 1
+        begin(used[0] + early)
         return dot(x, weight[pl.ds(pl.multiple_of(u * width, width), width), :])
 
-    cache_copy.wait()
-    for j in range(here):
-        pairs[j] = cache[j].reshape(pairs.shape[1], pairs.shape[2])
+
+    for copy in small:
+        copy.wait()
+
+    def mask_of(side_rows, a):
+        lane = iota((rows, HEAD), 1)
+        picked = jnp.where(lane == side * owned + a, masks[side_rows].astype(F32), 0.0)
+        return jnp.sum(picked, axis=1, keepdims=True)
+
+    def shrink(side_rows):
+        x = (raw[side_rows].astype(F32) * gain).astype(BF16)
+        total = jnp.zeros((rows, HEAD), F32)
+        for a in range(owned):
+            total = total + dot(x, down[a]) * mask_of(side_rows, a)
+        half_send[side_rows] = total
+
+    shrink(side)
 
     def squares_of(u):
         block = stats[u].astype(F32)
@@ -483,21 +505,7 @@
     def normed(block, row_factor, u):
         return (block.astype(F32) * row_factor * gain_of(u)).astype(BF16)
 
-    normed_mine = normed(raw[side], factor, me)
-    acc[...] = project(me, normed_mine)
-    for copy in small:
-        copy.wait()
-
-    def mask_of(side_rows, a):
-        lane = iota((rows, HEAD), 1)
-        picked = jnp.where(lane == side * owned + a, masks[side_rows].astype(F32), 0.0)
-        return jnp.sum(picked, axis=1, keepdims=True)
-
-    def shrink(side_rows, x):
-        total = jnp.zeros((rows, HEAD), F32)
-        for a in range(owned):
-            total = total + dot(x, down[a]) * mask_of(side_rows, a)
-        half_send[side_rows] = total
+    acc[...] = project(me, normed(raw[side], factor, me))
 
     def wait_x(u):
         remote(mine, gathered.at[u], x_send, x_recv.at[u], tp(sibling)).wait_recv()
@@ -522,12 +530,10 @@
         wait_x(u)
         add_block(u)
 
-    shrink(side, normed_mine)
     arrive(0)
     remote(masks.at[side], masks.at[other], peer_send.at[1], peer_recv.at[1], peer).wait_recv()
-    remote(totals.at[side], totals.at[other], peer_send.at[2], peer_recv.at[2], peer).wait_recv()
     remote(mine, raw.at[other], peer_send.at[0], peer_recv.at[0], peer).wait_recv()
-    shrink(other, normed(raw[other], factor_of(totals[other][0:1]), me))
+    shrink(other)
     half = remote(
         half_send.at[1 - core], half_recv, half_sem.at[0], half_sem.at[1], tp(sibling)
     )
@@ -557,7 +563,8 @@
             chip_sum.at[z], chip_sum.at[v], chip_send.at[0], chip_recv.at[v], tp(sibling)
         ).wait_recv()
         chip_total = chip_total + chip_sum[v].astype(F32)
-    ranks[core] = chip_total.astype(BF16)
+    remote(totals.at[side], totals.at[other], peer_send.at[2], peer_recv.at[2], peer).wait_recv()
+    ranks[core] = (chip_total * factor_of(totals[core][0:1])).astype(BF16)
     rank_copy = remote(
         ranks.at[core], ranks.at[core], rank_sem.at[0], rank_sem.at[1], tp(sibling)
     )
@@ -580,6 +587,8 @@
     lift_own[...] = lift(side)
     for i in range(2, last):
         arrive(i)
+        if i == last - 1:
+            cache_copy.start()
         add_same(i)
         add_other(i)
     lift_copy.wait_recv()
@@ -608,6 +617,11 @@
             )
         )
     heads_recv[me] = heads_send[me]
+    for u in wide_order:
+        wide_copy(u).start()
+    cache_copy.wait()
+    for j in range(here):
+        pairs[j] = cache[j].reshape(pairs.shape[1], pairs.shape[2])
 
     row = iota((pad, HEAD), 0)
     lane = iota((pad, HEAD), 1)
@@ -781,7 +795,7 @@
         )
 
     items = [(i, p) for i in range(chips) for p in range(parts)]
-    ahead = 2
+    ahead = 1
     for item in items[:ahead]:
         multiply(*item)
     for n, item in enumerate(items):

time: 73.7 us -> 68 us (0.923)
  Pallas kernels: 70.6 us -> 64.9 us
    pallas_call x1, Pallas kernels: 70.6 us -> 64.9 us  [fused(): pl.pallas_call(functools.partial(block_kernel, sizes), out_shape=jax.Shap...]
where the time goes in v3:
time: 68 us; the launch traced here: 67.8 us
  Pallas kernels  64.9 us (95%)
  local copies, waits for them, and re-layouts  2.87 us (4%)
    pallas_call x1, Pallas kernels, fused(): pl.pallas_call(functools.partial(block_kernel, sizes), out_shape=jax.Shap...  64.9 us
    unnamed x1, local copies, waits for them, and re-layouts  1.59 us

profile of v3, /device:TPU:0, one launch (start us, length us, event | category | flops | bytes accessed | tf_op | source)
XLA Modules:
  0.0 67.8 jit_solution(8942030569948251033)
XLA Ops:
  0.0 1.3 %reshape.6.gain_ref = bf16[1,1024]{1,0:T(2,128)(2,1)} reshape(bf16[1024]{0:T(1024)(128)(2,1)} %param.15) | data formatting | bytes 4096 | tf_op jit(solution)/shard_map/reshape | solution.py:915
  1.3 64.9 %shard_map.136 = bf16[2,40,1024]{2,1,0:T(8,128)(2,1)} custom-call(bf16[2,40,1024]{2,1,0:T(8,128)(2,1)} %tokens_ref.1, bf16[1,1024]{1,0:T(2,128)(2,1)} %reshape.6.gain_ref, s32[1,40]{1,0:T(1,128)} %bitcast.1, s32[2,3]{1,0:T(2,128)} %ids_ref.1, s32[8]{0:T(128)} %table_ref.1, s32[5]{0:T(128)} %length_ref.1, bf16[8192,1024]{1,0:T(8,128)(2,1)} %query_w.1, ...), custom_call_target="tpu_custom_call" | custom-call | tf_op jit(solution)/shard_map/pallas_call | solution.py:848
  66.2 1.6 %copy.16 = bf16[2,40,1024]{2,1,0:T(8,128)(2,1)} copy(bf16[2,40,1024]{2,1,0:T(8,128)(2,1)} %shard_map.136) | data formatting | bytes 327680

commit v4 on v3

--- a/solution.py
+++ b/solution.py
@@ -332,20 +332,25 @@
         span = pl.ds(pl.multiple_of(u * width, width), width)
         return pltpu.make_async_copy(out_w.at[:, span], wide_out.at[u], wide_sem.at[u])
 
-    small = [pltpu.make_async_copy(down_hbm, down, small_sem.at[0])]
+    small = []
     for a in range(owned):
         small.append(
             pltpu.make_async_copy(
+                down_hbm.at[a], down.at[:, pl.ds(a * HEAD, HEAD)], small_sem.at[0, a]
+            )
+        )
+        small.append(
+            pltpu.make_async_copy(
                 up_query_hbm.at[a],
-                up.at[a, pl.ds(0, HEAD // 2), pl.ds(0, columns)],
-                small_sem.at[1 + a],
+                up.at[pl.ds(a * HEAD, HEAD // 2), pl.ds(0, columns)],
+                small_sem.at[1, a],
             )
         )
         small.append(
             pltpu.make_async_copy(
                 up_value_hbm.at[a],
-                up.at[a, pl.ds(HEAD // 2, HEAD // 2), pl.ds(columns, HEAD)],
-                small_sem.at[1 + owned + a],
+                up.at[pl.ds(a * HEAD + HEAD // 2, HEAD // 2), pl.ds(columns, HEAD)],
+                small_sem.at[2, a],
             )
         )
     order = [me, sibling]
@@ -384,7 +389,7 @@
     high = square.astype(BF16).astype(F32)
     middle = (square - high).astype(BF16).astype(F32)
     low = square - high - middle
-    gain = gain_ref[...].astype(F32)
+    gain = gain_ref[...].astype(F32).reshape(1, width)
     gain_rows = width // HEAD
     stats[me] = jnp.concatenate(
         [gain[:, i * HEAD : (i + 1) * HEAD] for i in range(gain_rows)]
@@ -440,10 +445,10 @@
     begin(early)
 
     for a in range(owned):
-        up[a, pl.ds(HEAD // 2, HEAD // 2), pl.ds(0, columns)] = jnp.zeros(
+        up[pl.ds(a * HEAD + HEAD // 2, HEAD // 2), pl.ds(0, columns)] = jnp.zeros(
             (HEAD // 2, columns), BF16
         )
-        up[a, pl.ds(0, HEAD // 2), pl.ds(columns, HEAD)] = jnp.zeros((HEAD // 2, HEAD), BF16)
+        up[pl.ds(a * HEAD, HEAD // 2), pl.ds(columns, HEAD)] = jnp.zeros((HEAD // 2, HEAD), BF16)
 
     used = [0]
 
@@ -463,14 +468,12 @@
         picked = jnp.where(lane == side * owned + a, masks[side_rows].astype(F32), 0.0)
         return jnp.sum(picked, axis=1, keepdims=True)
 
-    def shrink(side_rows):
-        x = (raw[side_rows].astype(F32) * gain).astype(BF16)
+    def shrink(side_rows, x):
+        every = dot(x, down[...])
         total = jnp.zeros((rows, HEAD), F32)
         for a in range(owned):
-            total = total + dot(x, down[a]) * mask_of(side_rows, a)
+            total = total + every[:, a * HEAD : (a + 1) * HEAD] * mask_of(side_rows, a)
         half_send[side_rows] = total
-
-    shrink(side)
 
     def squares_of(u):
         block = stats[u].astype(F32)
@@ -505,7 +508,9 @@
     def normed(block, row_factor, u):
         return (block.astype(F32) * row_factor * gain_of(u)).astype(BF16)
 
-    acc[...] = project(me, normed(raw[side], factor, me))
+    normed_mine = normed(raw[side], factor, me)
+    shrink(side, normed_mine)
+    acc[...] = project(me, normed_mine)
 
     def wait_x(u):
         remote(mine, gathered.at[u], x_send, x_recv.at[u], tp(sibling)).wait_recv()
@@ -533,7 +538,8 @@
     arrive(0)
     remote(masks.at[side], masks.at[other], peer_send.at[1], peer_recv.at[1], peer).wait_recv()
     remote(mine, raw.at[other], peer_send.at[0], peer_recv.at[0], peer).wait_recv()
-    shrink(other)
+    remote(totals.at[side], totals.at[other], peer_send.at[2], peer_recv.at[2], peer).wait_recv()
+    shrink(other, normed(raw[other], factor_of(totals[other][0:1]), me))
     half = remote(
         half_send.at[1 - core], half_recv, half_sem.at[0], half_sem.at[1], tp(sibling)
     )
@@ -563,8 +569,7 @@
             chip_sum.at[z], chip_sum.at[v], chip_send.at[0], chip_recv.at[v], tp(sibling)
         ).wait_recv()
         chip_total = chip_total + chip_sum[v].astype(F32)
-    remote(totals.at[side], totals.at[other], peer_send.at[2], peer_recv.at[2], peer).wait_recv()
-    ranks[core] = (chip_total * factor_of(totals[core][0:1])).astype(BF16)
+    ranks[core] = chip_total.astype(BF16)
     rank_copy = remote(
         ranks.at[core], ranks.at[core], rank_sem.at[0], rank_sem.at[1], tp(sibling)
     )
@@ -576,10 +581,8 @@
 
     def lift(side_rows):
         rank = ranks[side_rows].astype(F32)
-        total = jnp.zeros((rows, columns + HEAD), F32)
-        for a in range(owned):
-            total = total + dot((rank * mask_of(side_rows, a)).astype(BF16), up[a])
-        return total
+        picked = [(rank * mask_of(side_rows, a)).astype(BF16) for a in range(owned)]
+        return dot(jnp.concatenate(picked, axis=1), up[...])
 
     lift_send[...] = lift(other).astype(BF16)
     lift_copy = remote(lift_send, lift_recv, lift_sem.at[0], lift_sem.at[1], peer)
@@ -853,8 +856,8 @@
         scratch_shapes=[
             vmem((T * width, span + HEAD), BF16),
             vmem((T, columns, width), BF16),
-            vmem(adapter_down_maps.shape, BF16),
-            vmem((owned, HEAD, span), BF16),
+            vmem((width, owned * HEAD), BF16),
+            vmem((owned * HEAD, span), BF16),
             vmem(key_value_cache.shape, BF16),
             vmem((here, count, KV_HEADS * HEAD), BF16),
             vmem((T, rows, width), BF16),
@@ -883,7 +886,7 @@
             vmem((2, chips, 2, rows, width // 2), BF16),
             dma((3, T)),
             dma((T,)),
-            dma((1 + 2 * owned,)),
+            dma((3, owned)),
             dma(()),
             dma(()),
             dma((T,)),
@@ -912,7 +915,7 @@
         ),
     )(
         tokens,
-        input_norm_gain.reshape(1, width),
+        input_norm_gain,
         request_adapter_entry.reshape(1, requests),
         group_adapter_ids,
         adapter_slot_table,

time: 68 us -> 66.6 us (0.979)
  local copies, waits for them, and re-layouts: 2.87 us -> 1.59 us
    reshape x1 -> x0, local copies, waits for them, and re-layouts: 1.28 us -> none  [fused(): input_norm_gain.reshape(1, width)]
where the time goes in v4:
time: 66.6 us; the launch traced here: 66.3 us
  Pallas kernels  64.7 us (97%)
  local copies, waits for them, and re-layouts  1.59 us (2%)
    pallas_call x1, Pallas kernels, fused(): pl.pallas_call(functools.partial(block_kernel, sizes), out_shape=jax.Shap...  64.7 us
    unnamed x1, local copies, waits for them, and re-layouts  1.59 us

profile of v4, /device:TPU:0, one launch (start us, length us, event | category | flops | bytes accessed | tf_op | source)
XLA Modules:
  0.0 66.3 jit_solution(16384444829222448799)
XLA Ops:
  0.0 64.7 %shard_map.136 = bf16[2,40,1024]{2,1,0:T(8,128)(2,1)} custom-call(bf16[2,40,1024]{2,1,0:T(8,128)(2,1)} %tokens_ref.1, bf16[1024]{0:T(1024)(128)(2,1)} %gain_ref.1, s32[1,40]{1,0:T(1,128)} %bitcast.1, s32[2,3]{1,0:T(2,128)} %ids_ref.1, s32[8]{0:T(128)} %table_ref.1, s32[5]{0:T(128)} %length_ref.1, bf16[8192,1024]{1,0:T(8,128)(2,1)} %query_w.1, ...), custom_call_target="tpu_custom_call" | custom-call | tf_op jit(solution)/shard_map/pallas_call | solution.py:851
  64.7 1.6 %copy.16 = bf16[2,40,1024]{2,1,0:T(8,128)(2,1)} copy(bf16[2,40,1024]{2,1,0:T(8,128)(2,1)} %shard_map.136) | data formatting | bytes 327680
